TPU v7x, 32 devices: a whole 2x2x4 slice. The times are simulated.
32 devices in a mesh: member: 2 (over core), tile: 16 (over z, y, x).
Axes of the slice: x: 2, y: 2, z: 4, core: 2. Of those that a mesh axis runs over, the one named last changes fastest.
Arguments:
- winds: bfloat16 [8, 4, 2, 256, 2048], P('member', None, None, 'tile'), may hold values from -6 to 6
Outputs:
- critical_density: float32 [4, 256, 2048], P(None, 'tile', 'member')
All inputs are finite; a program needn't handle non-finite values.
Results may differ from a plain program's by a relative error of at most 0.0003.
Values may be sent and summed in bfloat16 or wider, within the bound.
A program may use at most 128 MiB of HBM per device.

v0:
```python
import jax
import jax.numpy as jnp
from jax import lax
from jax.sharding import PartitionSpec as P

ridge = 0.1


def with_halo(array, sides, width):
    for axis, dim in sides:
        count, length = (lax.axis_size(axis), array.shape[dim])
        up = [(i, (i + 1) % count) for i in range(count - 1)]
        down = [(j, i) for i, j in up]
        last = lax.slice_in_dim(array, length - width, length, axis=dim)
        leading = lax.slice_in_dim(array, 0, width, axis=dim)
        before = lax.ppermute(last, axis, up)
        after = lax.ppermute(leading, axis, down)
        array = jnp.concatenate([before, array, after], axis=dim)
    return array


def density(extended, count):
    rows = extended[:, :, :-2] + extended[:, :, 1:-1] + extended[:, :, 2:]
    pooled = rows[..., :-2] + rows[..., 1:-1] + rows[..., 2:]
    mean_x = pooled[0] / count
    mean_y = pooled[1] / count
    cxx = pooled[2] / count - mean_x * mean_x + ridge
    cxy = pooled[3] / count - mean_x * mean_y
    cyy = pooled[4] / count - mean_y * mean_y + ridge
    lower_a = jnp.sqrt(cxx)
    lower_b = cxy / lower_a
    lower_c = jnp.sqrt(cyy - lower_b * lower_b)
    first = -mean_x / lower_a
    second = (-mean_y - lower_b * first) / lower_c
    return jnp.exp(-0.5 * (first * first + second * second)) / (2.0 * jnp.pi * lower_a * lower_c)


def per_device(winds):
    members_here = winds.shape[0]
    count = 9.0 * members_here * lax.axis_size("member")
    extended = with_halo(winds, (("tile", 3),), 1).astype(jnp.float32)
    energy = 0.5 * (extended[:, :, 0] * extended[:, :, 0] + extended[:, :, 1] * extended[:, :, 1])
    inner = energy[:, :, 1:-1]
    grad_x = 0.5 * (jnp.roll(inner, -1, axis=3) - jnp.roll(inner, 1, axis=3))
    grad_y = 0.5 * (energy[:, :, 2:] - energy[:, :, :-2])
    partial_sums = jnp.stack(
        [
            jnp.sum(grad_x, axis=0),
            jnp.sum(grad_y, axis=0),
            jnp.sum(grad_x * grad_x, axis=0),
            jnp.sum(grad_x * grad_y, axis=0),
            jnp.sum(grad_y * grad_y, axis=0),
        ]
    )
    totals = lax.psum(partial_sums, "member")
    width = totals.shape[3] // lax.axis_size("member")
    wrapped = jnp.concatenate([totals[..., -1:], totals, totals[..., :1]], axis=3)
    offset = lax.axis_index("member") * width
    slab = lax.dynamic_slice_in_dim(wrapped, offset, width + 2, 3)
    padded = with_halo(slab, (("tile", 2),), 1)
    return density(padded, count)


def solution(mesh):
    return jax.shard_map(
        per_device,
        mesh=mesh,
        in_specs=(P("member", None, None, "tile", None),),
        out_specs=P(None, "tile", "member"),
        check_vma=False,
    )
```

profile of v0, /device:TPU:0, one launch (start us, length us, event | category | flops | bytes accessed | tf_op | source)
XLA Modules:
  0.0 75.6 jit_solution(1664617808091114538)
XLA Ops:
  6.5 2.2 %fusion.20 = (bf16[4,4,2,1,2048]{4,3,2,1,0:T(2,128)(2,1)S(1)}, bf16[4,4,2,1,2048]{4,3,2,1,0:T(2,128)(2,1)S(1)}) fusion(bf16[4,4,2,16,2048]{4,3,2,1,0:T(8,128)(2,1)} %param.1), kind=kLoop, calls=%fused_computation.46 | loop fusion | bytes 524288 | tf_op jit(solution)/shard_map/slice | solution.py:14
  9.0 4.8 %collective-permute-start = (bf16[4,4,2,1,2048]{4,1,3,2,0:T(4,128)(2,1)S(1)}, bf16[4,4,2,1,2048]{4,1,3,2,0:T(4,128)(2,1)S(1)}, u32[]{:S(2)}, u32[]{:S(2)}) collective-permute-start(bf16[4,4,2,1,2048]{4,1,3,2,0:T(4,128)(2,1)S(1)} %copy.6), channel_id=1, source_target_pairs={{0,1},{1,2},{2,3},{3,4},{4,5},{5,6},{6,7},{7,8},{8,9},{9,10},{10,1... | collective-permute-start | bytes 393224 | tf_op jit(solution)/shard_map/ppermute | solution.py:16
  14.0 1.3 %collective-permute-start.1 = (bf16[4,4,2,1,2048]{4,1,3,2,0:T(4,128)(2,1)S(1)}, bf16[4,4,2,1,2048]{4,1,3,2,0:T(4,128)(2,1)S(1)}, u32[]{:S(2)}, u32[]{:S(2)}) collective-permute-start(bf16[4,4,2,1,2048]{4,1,3,2,0:T(4,128)(2,1)S(1)} %copy.7), channel_id=1, source_target_pairs={{1,0},{2,1},{3,2},{4,3},{5,4},{6,5},{7,6},{8,7},{9,8},{10,9},{11,1... | collective-permute-start | bytes 393224 | tf_op jit(solution)/shard_map/ppermute | solution.py:17
  15.3 1.2 %collective-permute-done = bf16[4,4,2,1,2048]{4,1,3,2,0:T(4,128)(2,1)S(1)} collective-permute-done((bf16[4,4,2,1,2048]{4,1,3,2,0:T(4,128)(2,1)S(1)}, bf16[4,4,2,1,2048]{4,1,3,2,0:T(4,128)(2,1)S(1)}, u32[]{:S(2)}, u32[]{:S(2)}) %collective-permute-start) | collective-permute-done | bytes 131104 | tf_op jit(solution)/shard_map/ppermute | solution.py:16
  16.6 0.2 copy.4
  16.8 4.5 %collective-permute-done.1 = bf16[4,4,2,1,2048]{4,1,3,2,0:T(4,128)(2,1)S(1)} collective-permute-done((bf16[4,4,2,1,2048]{4,1,3,2,0:T(4,128)(2,1)S(1)}, bf16[4,4,2,1,2048]{4,1,3,2,0:T(4,128)(2,1)S(1)}, u32[]{:S(2)}, u32[]{:S(2)}) %collective-permute-start.1) | collective-permute-done | bytes 131104 | tf_op jit(solution)/shard_map/ppermute | solution.py:17
  21.3 0.2 copy.5
  21.5 1.4 %maximum_convert_fusion = f32[4,4,2,18,2048]{4,3,2,1,0:T(8,128)S(1)} fusion(bf16[4,4,2,1,2048]{4,3,2,1,0:T(2,128)(2,1)S(1)} %copy.5, bf16[4,4,2,16,2048]{4,3,2,1,0:T(8,128)(2,1)S(1)} %copy-done.1, bf16[4,4,2,1,2048]{4,3,2,1,0:T(2,128)(2,1)S(1)} %copy.4), kind=kLoop, calls=%fused_computation.5 | loop fusion | flops 7077888 | bytes 7077888 | tf_op jit(solution)/shard_map/convert_element_type | solution.py:41
  23.0 0.6 fusion.2
  23.6 1.0 %fusion.18 = (f32[4,4,16,2047]{3,2,1,0:T(8,128)S(1)}, f32[4,4,16,2047]{3,2,1,0:T(8,128)S(1)}) fusion(f32[4,4,18,2048]{3,2,1,0:T(8,128)S(1)} %fusion.2), kind=kLoop, calls=%fused_computation.44 | loop fusion | bytes 8384512 | tf_op jit(solution)/shard_map/jit(_roll_static)/slice | solution.py:44
  24.7 1.1 %multiply_reduce_fusion = (f32[4,16,2048]{2,1,0:T(8,128)S(1)}, f32[4,16,2048]{2,1,0:T(8,128)S(1)}, f32[4,16,2048]{2,1,0:T(8,128)S(1)}, f32[4,16,2048]{2,1,0:T(8,128)S(1)}, f32[4,16,2048]{2,1,0:T(8,128)S(1)}) fusion(f32[4,4,18,2048]{3,2,1,0:T(8,128)S(1)} %fusion.2, f32[4,4,16,2047]{3,2,1,0:T(8,128)S(1)} %get-tuple-element.12, ...), kind=kLoop, calls=%fused_computation.10 | loop fusion | flops 6684672 | bytes 11010048 | tf_op jit(solution)/shard_map/reduce_sum | solution.py:52
  26.0 1.5 %copy-done = f32[5,4,16,2048]{3,2,1,0:T(8,128)} copy-done((f32[5,4,16,2048]{3,2,1,0:T(8,128)}, f32[5,4,16,2048]{3,2,1,0:T(8,128)S(1)}, u32[]{:S(2)}) %copy-start) | copy-done | bytes 2621464
  27.6 23.9 %all-reduce.2.cloned.1.call-done = f32[5,4,16,2048]{3,2,1,0:T(8,128)} async-done(((f32[5,4,16,2048]{3,2,1,0:T(8,128)}), f32[5,4,16,2048]{3,2,1,0:T(8,128)}) %all-reduce.2.cloned.1.call-update) | async-done | bytes 2621456 | tf_op jit(solution)/shard_map/psum | solution.py:55
  51.5 1.1 %fusion.19 = (f32[5,4,16,1]{3,2,1,0:T(8,128)S(1)}, f32[5,4,16,1]{3,2,1,0:T(8,128)S(1)}) fusion(f32[5,4,16,2048]{3,2,1,0:T(8,128)} %all-reduce.2.cloned.1.call-done), kind=kLoop, calls=%fused_computation.45 | loop fusion | bytes 5120 | tf_op jit(solution)/shard_map/slice | solution.py:57
  52.6 3.2 %concatenate.24 = f32[5,4,16,2050]{3,2,1,0:T(8,128)S(1)} concatenate(f32[5,4,16,1]{3,2,1,0:T(8,128)S(1)} %get-tuple-element.17, f32[5,4,16,2048]{3,2,1,0:T(8,128)} %all-reduce.2.cloned.1.call-done, f32[5,4,16,1]{3,2,1,0:T(8,128)S(1)} %get-tuple-element.16), dimensions={3} | concatenate | bytes 5248000 | tf_op jit(solution)/shard_map/concatenate | solution.py:57
  55.8 0.5 constant_dynamic-slice_fusion.1
  56.3 3.6 %collective-permute-start.2 = (f32[5,4,1,1026]{3,2,1,0:T(1,128)S(1)}, f32[5,4,1,1026]{3,2,1,0:T(1,128)S(1)}, u32[]{:S(2)}, u32[]{:S(2)}) collective-permute-start(f32[5,4,1,1026]{3,2,1,0:T(1,128)S(1)} %get-tuple-element.14), channel_id=1, source_target_pairs={{0,1},{1,2},{2,3},{3,4},{4,5},{5,6},{6,7},{7,8},{8,9},{9,10},{10,1... | collective-permute-start | bytes 246248 | tf_op jit(solution)/shard_map/ppermute | solution.py:16
  60.0 1.3 %collective-permute-start.3 = (f32[5,4,1,1026]{3,2,1,0:T(1,128)S(1)}, f32[5,4,1,1026]{3,2,1,0:T(1,128)S(1)}, u32[]{:S(2)}, u32[]{:S(2)}) collective-permute-start(f32[5,4,1,1026]{3,2,1,0:T(1,128)S(1)} %get-tuple-element.15), channel_id=1, source_target_pairs={{1,0},{2,1},{3,2},{4,3},{5,4},{6,5},{7,6},{8,7},{9,8},{10,9},{11,1... | collective-permute-start | bytes 246248 | tf_op jit(solution)/shard_map/ppermute | solution.py:17
  61.3 0.5 constant_dynamic-slice_fusion.2
  61.7 0.6 collective-permute-done.2
  62.3 4.1 %collective-permute-done.3 = f32[5,4,1,1026]{3,2,1,0:T(1,128)S(1)} collective-permute-done((f32[5,4,1,1026]{3,2,1,0:T(1,128)S(1)}, f32[5,4,1,1026]{3,2,1,0:T(1,128)S(1)}, u32[]{:S(2)}, u32[]{:S(2)}) %collective-permute-start.3) | collective-permute-done | bytes 82112 | tf_op jit(solution)/shard_map/ppermute | solution.py:17
  66.4 0.4 fusion.5
  66.9 0.7 slice_add_fusion
  67.6 1.1 %divide_bitcast_fusion = f32[4,16,1024]{2,1,0:T(8,128)} fusion(f32[5,4,16,1024]{3,2,1,0:T(8,128)S(1)} %slice_add_fusion), kind=kLoop, calls=%fused_computation.38 | loop fusion | flops 1900544 | bytes 1572864 | tf_op jit(solution)/shard_map/div | solution.py:35
  (13 shorter events, 0.7 us)
Async XLA Ops:
  6.5 15.0 %copy-start.1 = (bf16[4,4,2,16,2048]{4,3,2,1,0:T(8,128)(2,1)S(1)}, bf16[4,4,2,16,2048]{4,3,2,1,0:T(8,128)(2,1)}, u32[]{:S(2)}) copy-start(bf16[4,4,2,16,2048]{4,3,2,1,0:T(8,128)(2,1)} %param.1) | copy-start | bytes 6291460
  6.5 45.0 %all-reduce.2.cloned.1.call-start = ((), (), s32[]{:S(2)}) async-start(), calls=%async_computation | async-start | bytes 5242880 | tf_op jit(solution)/shard_map/psum | solution.py:55
  9.0 7.6 %collective-permute-start = (bf16[4,4,2,1,2048]{4,1,3,2,0:T(4,128)(2,1)S(1)}, bf16[4,4,2,1,2048]{4,1,3,2,0:T(4,128)(2,1)S(1)}, u32[]{:S(2)}, u32[]{:S(2)}) collective-permute-start(bf16[4,4,2,1,2048]{4,1,3,2,0:T(4,128)(2,1)S(1)} %copy.6), channel_id=1, source_target_pairs={{0,1},{1,2},{2,3},{3,4},{4,5},{5,6},{6,7},{7,8},{8,9},{9,10},{10,1... | collective-permute-start | bytes 393224 | tf_op jit(solution)/shard_map/ppermute | solution.py:16
  14.0 7.3 %collective-permute-start.1 = (bf16[4,4,2,1,2048]{4,1,3,2,0:T(4,128)(2,1)S(1)}, bf16[4,4,2,1,2048]{4,1,3,2,0:T(4,128)(2,1)S(1)}, u32[]{:S(2)}, u32[]{:S(2)}) collective-permute-start(bf16[4,4,2,1,2048]{4,1,3,2,0:T(4,128)(2,1)S(1)} %copy.7), channel_id=1, source_target_pairs={{1,0},{2,1},{3,2},{4,3},{5,4},{6,5},{7,6},{8,7},{9,8},{10,9},{11,1... | collective-permute-start | bytes 393224 | tf_op jit(solution)/shard_map/ppermute | solution.py:17
  26.0 1.5 %copy-start = (f32[5,4,16,2048]{3,2,1,0:T(8,128)}, f32[5,4,16,2048]{3,2,1,0:T(8,128)S(1)}, u32[]{:S(2)}) copy-start(f32[5,4,16,2048]{3,2,1,0:T(8,128)S(1)} %bitcast_dynamic-update-slice_fusion) | copy-start | bytes 7864324
  56.3 6.0 %collective-permute-start.2 = (f32[5,4,1,1026]{3,2,1,0:T(1,128)S(1)}, f32[5,4,1,1026]{3,2,1,0:T(1,128)S(1)}, u32[]{:S(2)}, u32[]{:S(2)}) collective-permute-start(f32[5,4,1,1026]{3,2,1,0:T(1,128)S(1)} %get-tuple-element.14), channel_id=1, source_target_pairs={{0,1},{1,2},{2,3},{3,4},{4,5},{5,6},{6,7},{7,8},{8,9},{9,10},{10,1... | collective-permute-start | bytes 246248 | tf_op jit(solution)/shard_map/ppermute | solution.py:16
  60.0 6.5 %collective-permute-start.3 = (f32[5,4,1,1026]{3,2,1,0:T(1,128)S(1)}, f32[5,4,1,1026]{3,2,1,0:T(1,128)S(1)}, u32[]{:S(2)}, u32[]{:S(2)}) collective-permute-start(f32[5,4,1,1026]{3,2,1,0:T(1,128)S(1)} %get-tuple-element.15), channel_id=1, source_target_pairs={{1,0},{2,1},{3,2},{4,3},{5,4},{6,5},{7,6},{8,7},{9,8},{10,9},{11,1... | collective-permute-start | bytes 246248 | tf_op jit(solution)/shard_map/ppermute | solution.py:17
Sparse Core Ops, SparseCore 0:
  27.7 23.7 all-reduce.1
where the time goes:
time: 76.2 us; the launch traced here: 75.6 us
  waiting for transfers between devices  34.4 us (45%)
  between operations  13.6 us (18%)
  local copies, waits for them, and re-layouts  11.1 us (15%)
  starting transfers between devices  11.1 us (15%)
  other arithmetic  5.4 us (7%)
    psum x1, waiting for transfers between devices, per_device(): totals = lax.psum(partial_sums, 'member')  23.9 us
    ppermute x2, waiting for transfers between devices, with_halo(): after = lax.ppermute(leading, axis, down)  8.65 us
    ppermute x2, starting transfers between devices, with_halo(): before = lax.ppermute(last, axis, up)  8.49 us
    concatenate x1, local copies, waits for them, and re-layouts, per_device(): jnp.concatenate([totals[..., -1:], totals, totals[..., :1]], axis=3)  3.24 us
    slice x2, local copies, waits for them, and re-layouts, with_halo(): last = lax.slice_in_dim(array, length - width, length, axis=dim)  2.7 us
    ppermute x2, starting transfers between devices, with_halo(): after = lax.ppermute(leading, axis, down)  2.58 us
    unnamed x10, local copies, waits for them, and re-layouts  2.02 us
    ppermute x2, waiting for transfers between devices, with_halo(): before = lax.ppermute(last, axis, up)  1.85 us
  transfers between devices with their start and end apart: 5, of which 5 were waited for; matrix products, arithmetic and copies ran while one was open for 1% of the time, Pallas kernels for 0%

commit v1 on v0

v1 whole, which is shorter than its diff:
```python
import functools

import jax
import jax.numpy as jnp
from jax import lax
from jax.experimental import pallas as pl
from jax.experimental.pallas import tpu as pltpu
from jax.sharding import PartitionSpec as P

RIDGE = 0.1
MESH = pl.DeviceIdType.MESH
LANES = 128


def row_order(size, rows):
    out = lax.broadcasted_iota(jnp.int32, (size, size), 0)
    src = lax.broadcasted_iota(jnp.int32, (size, size), 1)
    wanted = ((out % 8) * 2 + (out // 8) % 2) * rows + out // 16
    return jnp.where(src == wanted, 1.0, 0.0).astype(jnp.bfloat16)


def pick(matrix, block):
    return jnp.dot(matrix, block, preferred_element_type=jnp.float32)


def west(x):
    return pltpu.roll(x, 1, 1)


def east(x):
    return pltpu.roll(x, x.shape[1] - 1, 1)


def fold(x, half):
    shape = (8, LANES)
    near = lax.broadcasted_iota(jnp.int32, shape, 1) < LANES // 2
    edge = x[:, 2 * half :]
    low = jnp.concatenate(
        [x[:, :half], jnp.where(near, x[:, half : half + LANES], edge)], axis=1
    )
    high = jnp.concatenate(
        [x[:, half : 2 * half], jnp.where(near, edge, x[:, half - LANES : half])], axis=1
    )
    upper = lax.broadcasted_iota(jnp.int32, low.shape, 0) < 4
    return jnp.where(upper, low, high) + pltpu.roll(jnp.where(upper, high, low), 4, 0)


def pool(x, half):
    return (x + west(x) + east(x))[:, :half]


def density(sum_x, sum_y, sum_xx, sum_xy, sum_yy, count):
    mean_x = sum_x * (0.25 / count)
    mean_y = sum_y * (0.25 / count)
    cxx = sum_xx * (0.0625 / count) - mean_x * mean_x + RIDGE
    cxy = sum_xy * (0.0625 / count) - mean_x * mean_y
    cyy = sum_yy * (0.0625 / count) - mean_y * mean_y + RIDGE
    inv_a = lax.rsqrt(cxx)
    lower_b = cxy * inv_a
    inv_c = lax.rsqrt(cyy - lower_b * lower_b)
    first = -mean_x * inv_a
    second = (-mean_y - lower_b * first) * inv_c
    return jnp.exp(-0.5 * (first * first + second * second)) * (inv_a * inv_c) * (0.5 / jnp.pi)


def kernel(
    n, tiles, rows, pairs, count,
    winds, out,
    own, slab, halo, edge_out, edge_in, energy, first, xx, xy, yy, ends_out, ends_in, dens,
    own_sem, here_sem, slab_send, slab_recv, halo_send, halo_recv,
    edge_send, edge_recv, ends_send, ends_recv,
):
    me, tile = lax.axis_index("member"), lax.axis_index("tile")
    lons = own.shape[1]
    width = lons // n
    half = width // 2
    size = 16 * rows
    has = (tile > 0, tile < tiles - 1)
    beside = (tile - 1, tile + 1)

    def peer(step):
        return lax.rem(me + step, n)

    def columns(start, length):
        return pl.ds(pl.multiple_of(start, LANES), length)

    load = pltpu.make_async_copy(winds, own, own_sem)
    load.start()
    here = pltpu.make_async_copy(
        winds.at[:, columns(me * width, width)], slab.at[0, :, pl.ds(0, width)], here_sem
    )
    here.start()

    barrier = pltpu.get_barrier_semaphore()
    for step in range(1, n):
        pl.semaphore_signal(
            barrier, inc=1, device_id={"member": peer(step), "tile": tile}, device_id_type=MESH
        )
    for side in range(2):
        @pl.when(has[side])
        def _():
            for step in range(n):
                pl.semaphore_signal(
                    barrier, inc=1, device_id={"member": peer(step), "tile": beside[side]},
                    device_id_type=MESH,
                )

    order = row_order(size, rows)
    ends = jnp.concatenate([order[:16], order[size - 16 :]], axis=0)
    load.wait()
    near = lax.broadcasted_iota(jnp.int32, (1, LANES), 1) < LANES // 2
    for q in range(pairs):
        packed = pick(ends, own[q * size : (q + 1) * size, :]).astype(jnp.bfloat16)
        for side in range(2):
            ends_rows = packed[side * 16 : (side + 1) * 16]
            edge_out[side, n, q * 16 : (q + 1) * 16, :lons] = ends_rows
    for step in range(n):
        to = peer(step)
        right = columns(lax.rem(to + 1, n) * width, LANES)
        left = columns(lax.rem(to + n - 1, n) * width + width - LANES, LANES)
        for side in range(2):
            edge_out[side, step, :, :width] = edge_out[side, n, :, columns(to * width, width)]
            edge_out[side, step, :, width : width + LANES] = jnp.where(
                near, edge_out[side, n, :, right], edge_out[side, n, :, left]
            )

    sides = jnp.where(has[0], 1, 0) + jnp.where(has[1], 1, 0)
    pl.semaphore_wait(barrier, n - 1 + n * sides)

    def edge_copy(side, step):
        return pltpu.make_async_remote_copy(
            src_ref=edge_out.at[side, step, :, pl.ds(0, width + LANES)],
            dst_ref=edge_in.at[1 - side, step],
            send_sem=edge_send.at[side, step],
            recv_sem=edge_recv.at[1 - side, step],
            device_id={"member": peer(step), "tile": beside[side]},
            device_id_type=MESH,
        )

    def edge_arrival(side, step):
        return pltpu.make_async_remote_copy(
            src_ref=edge_out.at[side, step, :, pl.ds(0, width + LANES)],
            dst_ref=edge_in.at[side, step],
            send_sem=edge_send.at[side, step],
            recv_sem=edge_recv.at[side, step],
            device_id={"member": peer(step), "tile": beside[side]},
            device_id_type=MESH,
        )

    for side in range(2):
        @pl.when(has[side])
        def _():
            for step in range(n):
                edge_copy(side, step).start()

    slab_copies, halo_copies = [], []
    for step in range(1, n):
        device = {"member": peer(step), "tile": tile}
        copy = pltpu.make_async_remote_copy(
            src_ref=winds.at[:, columns(peer(step) * width, width)],
            dst_ref=slab.at[step, :, pl.ds(0, width)],
            send_sem=slab_send.at[step], recv_sem=slab_recv.at[step],
            device_id=device, device_id_type=MESH,
        )
        copy.start()
        slab_copies.append(copy)

    for step in range(n):
        to = peer(step)
        right = columns(lax.rem(to + 1, n) * width, LANES)
        left = columns(lax.rem(to + n - 1, n) * width + width - LANES, LANES)
        tile_columns = jnp.where(near, own[:, right], own[:, left])
        if step == 0:
            slab[0, :, width:] = tile_columns
            continue
        halo[step - 1] = tile_columns
        copy = pltpu.make_async_remote_copy(
            src_ref=halo.at[step - 1],
            dst_ref=slab.at[step, :, pl.ds(width, LANES)],
            send_sem=halo_send.at[step], recv_sem=halo_recv.at[step],
            device_id={"member": to, "tile": tile}, device_id_type=MESH,
        )
        copy.start()
        halo_copies.append(copy)

    chunk = 3 * LANES if (width + LANES) % (3 * LANES) == 0 else LANES
    for step in range(n):
        if step == 0:
            here.wait()
        else:
            slab_copies[step - 1].wait_recv()
            halo_copies[step - 1].wait_recv()
        for q in range(pairs):
            for c in range(0, width + LANES, chunk):
                block = slab[step, q * size : (q + 1) * size, c : c + chunk]
                parts = pick(order, block).reshape(rows, 2, 8, chunk)
                energy[step * pairs + q, 1 : rows + 1, :, c : c + chunk] = (
                    parts[:, 0] * parts[:, 0] + parts[:, 1] * parts[:, 1]
                )

    groups = n * pairs

    def moments(i):
        total = sum_xx = sum_xy = sum_yy = None
        for p in range(groups):
            e = energy[p, i]
            gx = east(e) - west(e)
            gy = energy[p, i + 1] - energy[p, i - 1]
            terms = (e, gx * gx, gx * gy, gy * gy)
            if p == 0:
                total, sum_xx, sum_xy, sum_yy = terms
            else:
                total, sum_xx, sum_xy, sum_yy = (
                    total + terms[0], sum_xx + terms[1], sum_xy + terms[2], sum_yy + terms[3]
                )
        first[i] = fold(total, half)
        xx[i] = fold(sum_xx, half)
        xy[i] = fold(sum_xy, half)
        yy[i] = fold(sum_yy, half)

    def outer(i):
        total = sum_xx = None
        for p in range(groups):
            e = energy[p, i]
            gx = east(e) - west(e)
            total, sum_xx = (e, gx * gx) if p == 0 else (total + e, sum_xx + gx * gx)
        first[i] = fold(total, half)
        xx[i] = fold(sum_xx, half)

    pl.loop(2, rows)(moments)

    for side in range(2):
        row = 0 if side == 0 else rows + 1

        @pl.when(has[side])
        def _():
            for step in range(n):
                edge_arrival(side, step).wait_recv()
                for q in range(pairs):
                    parts = edge_in[side, step, q * 16 : (q + 1) * 16, :].astype(jnp.float32)
                    energy[step * pairs + q, row] = parts[:8] * parts[:8] + parts[8:] * parts[8:]

        @pl.when(jnp.logical_not(has[side]))
        def _():
            for p in range(groups):
                energy[p, row] = jnp.zeros_like(energy[p, row])
            ends_in[side] = jnp.zeros_like(ends_in[side])

    def ends_copy(side, landing):
        return pltpu.make_async_remote_copy(
            src_ref=ends_out.at[side],
            dst_ref=ends_in.at[landing],
            send_sem=ends_send.at[side],
            recv_sem=ends_recv.at[landing],
            device_id={"member": me, "tile": beside[side]},
            device_id_type=MESH,
        )

    for side in range(2):
        row, inner, beyond = (1, 2, 0) if side == 0 else (rows, rows - 1, rows + 1)
        moments(row)
        outer(beyond)
        ends_out[side, 0] = pool(first[row + 1] - first[row - 1], half)
        ends_out[side, 1] = pool(xy[row], half)
        ends_out[side, 2] = pool(yy[row], half)

        @pl.when(has[side])
        def _():
            ends_copy(side, 1 - side).start()

    def x_sums(i):
        s = first[i - 1] + first[i] + first[i + 1]
        s = s + west(s) + east(s)
        return (east(s) - west(s))[:, :half], pool(xx[i - 1] + xx[i] + xx[i + 1], half)

    def inside(i):
        sum_x, sum_xx = x_sums(i)
        sum_y = pool(first[i + 2] + first[i + 1] - first[i - 1] - first[i - 2], half)
        sum_xy = pool(xy[i - 1] + xy[i] + xy[i + 1], half)
        sum_yy = pool(yy[i - 1] + yy[i] + yy[i + 1], half)
        dens[i - 1] = density(sum_x, sum_y, sum_xx, sum_xy, sum_yy, count)

    pl.loop(2, rows)(inside)

    for side in range(2):
        row, inner = (1, 2) if side == 0 else (rows, rows - 1)
        sum_x, sum_xx = x_sums(row)

        @pl.when(has[side])
        def _():
            ends_copy(side, side).wait_recv()

        sum_y = ends_out[side, 0] + pool(first[inner + 1] - first[inner - 1], half) + ends_in[side, 0]
        sum_xy = ends_out[side, 1] + pool(xy[inner], half) + ends_in[side, 1]
        sum_yy = ends_out[side, 2] + pool(yy[inner], half) + ends_in[side, 2]
        dens[row - 1] = density(sum_x, sum_y, sum_xx, sum_xy, sum_yy, count)

    levels = out.shape[0]
    for r in range(0, rows, 8):
        turned = jnp.swapaxes(dens[r : r + 8], 0, 1)
        out[:, r : r + 8, :half] = turned[:levels]
        out[:, r : r + 8, half:] = turned[levels:]

    for copy in slab_copies + halo_copies:
        copy.wait_send()
    for side in range(2):
        @pl.when(has[side])
        def _():
            for step in range(n):
                edge_copy(side, step).wait_send()
            ends_copy(side, 1 - side).wait_send()


def per_device(n, tiles, winds):
    members, levels, parts, rows, lons = winds.shape
    width = lons // n
    half = width // 2
    pairs = members // 2
    size = 16 * rows
    assert levels == 4 and parts == 2 and members % 2 == 0 and rows % 8 == 0 and half % LANES == 0
    count = 9.0 * members * n
    groups = n * pairs
    dma = pltpu.SemaphoreType.DMA
    return pl.pallas_call(
        functools.partial(kernel, n, tiles, rows, pairs, count),
        out_shape=jax.ShapeDtypeStruct((levels, rows, width), jnp.float32),
        in_specs=[pl.BlockSpec(memory_space=pl.ANY)],
        out_specs=pl.BlockSpec(memory_space=pltpu.VMEM),
        scratch_shapes=[
            pltpu.VMEM((pairs * size, lons), jnp.bfloat16),
            pltpu.VMEM((n, pairs * size, width + LANES), jnp.bfloat16),
            pltpu.VMEM((max(n - 1, 1), pairs * size, LANES), jnp.bfloat16),
            pltpu.VMEM((2, n + 1, pairs * 16, max(lons, width + LANES)), jnp.bfloat16),
            pltpu.VMEM((2, n, pairs * 16, width + LANES), jnp.bfloat16),
            pltpu.VMEM((groups, rows + 2, 8, width + LANES), jnp.float32),
            pltpu.VMEM((rows + 2, 8, half + LANES), jnp.float32),
            pltpu.VMEM((rows + 2, 8, half + LANES), jnp.float32),
            pltpu.VMEM((rows + 2, 8, half + LANES), jnp.float32),
            pltpu.VMEM((rows + 2, 8, half + LANES), jnp.float32),
            pltpu.VMEM((2, 3, 8, half), jnp.float32),
            pltpu.VMEM((2, 3, 8, half), jnp.float32),
            pltpu.VMEM((rows, 8, half), jnp.float32),
            dma, dma, dma((n,)), dma((n,)), dma((n,)), dma((n,)),
            dma((2, n)), dma((2, n)), dma((2,)), dma((2,)),
        ],
        compiler_params=pltpu.CompilerParams(
            collective_id=0, has_side_effects=True, vmem_limit_bytes=48 * 2**20
        ),
    )(winds.reshape(pairs * size, lons))


def solution(mesh):
    return jax.shard_map(
        functools.partial(per_device, mesh.shape["member"], mesh.shape["tile"]),
        mesh=mesh,
        in_specs=(P("member", None, None, "tile", None),),
        out_specs=P(None, "tile", "member"),
        check_vma=False,
    )
```

time: 76.2 us -> 18.4 us (0.24)
  the two profiles are of different devices: /device:TPU:0 before, /device:TPU:13 now
where the time goes in v1:
time: 18.4 us; the launch traced here: 18.3 us
  Pallas kernels  16 us (87%)
  local copies, waits for them, and re-layouts  2.3 us (12%)
    pallas_call x1, Pallas kernels, per_device(): pl.pallas_call(functools.partial(kernel, n, tiles, rows, pairs, count), o...  16 us
    unnamed x3, local copies, waits for them, and re-layouts  2.3 us

profile of v1, /device:TPU:13, one launch (start us, length us, event | category | flops | bytes accessed | tf_op | source)
XLA Modules:
  0.0 18.3 jit_solution(11302583090636779409)
XLA Ops:
  0.0 0.0 copy-start
  0.0 1.6 %copy-done = bf16[4,4,2,16,2048]{4,3,2,1,0:T(8,128)(2,1)S(1)} copy-done((bf16[4,4,2,16,2048]{4,3,2,1,0:T(8,128)(2,1)S(1)}, bf16[4,4,2,16,2048]{4,3,2,1,0:T(8,128)(2,1)}, u32[]{:S(2)}) %copy-start) | copy-done | bytes 2097176
  1.6 16.0 %shard_map.17 = f32[4,16,1024]{2,1,0:T(8,128)S(1)} custom-call(bf16[512,2048]{1,0:T(8,128)(2,1)S(1)} %bitcast.1), custom_call_target="tpu_custom_call" | custom-call | tf_op jit(solution)/shard_map/pallas_call | solution.py:324
  17.6 0.7 %copy.3 = f32[4,16,1024]{2,1,0:T(8,128)} copy(f32[4,16,1024]{2,1,0:T(8,128)S(1)} %shard_map.17) | data formatting | bytes 524288
Async XLA Ops:
  0.0 1.6 %copy-start = (bf16[4,4,2,16,2048]{4,3,2,1,0:T(8,128)(2,1)S(1)}, bf16[4,4,2,16,2048]{4,3,2,1,0:T(8,128)(2,1)}, u32[]{:S(2)}) copy-start(bf16[4,4,2,16,2048]{4,3,2,1,0:T(8,128)(2,1)} %param.1) | copy-start | bytes 6291460

commit v2 on v1

--- a/solution.py
+++ b/solution.py
@@ -66,9 +66,10 @@
 def kernel(
     n, tiles, rows, pairs, count,
     winds, out,
-    own, slab, halo, edge_out, edge_in, energy, first, xx, xy, yy, ends_out, ends_in, dens,
+    own, slab, halo, edge_all, edge_out, edge_in, energy, first, xx, xy, yy,
+    early_out, early_in, late_out, late_in, dens,
     own_sem, here_sem, slab_send, slab_recv, halo_send, halo_recv,
-    edge_send, edge_recv, ends_send, ends_recv,
+    edge_send, edge_recv, early_send, early_recv, late_send, late_recv,
 ):
     me, tile = lax.axis_index("member"), lax.axis_index("tile")
     lons = own.shape[1]
@@ -109,27 +110,38 @@
     ends = jnp.concatenate([order[:16], order[size - 16 :]], axis=0)
     load.wait()
     near = lax.broadcasted_iota(jnp.int32, (1, LANES), 1) < LANES // 2
+    lane = lax.broadcasted_iota(jnp.int32, (1, LANES), 1)
     for q in range(pairs):
         packed = pick(ends, own[q * size : (q + 1) * size, :]).astype(jnp.bfloat16)
         for side in range(2):
-            ends_rows = packed[side * 16 : (side + 1) * 16]
-            edge_out[side, n, q * 16 : (q + 1) * 16, :lons] = ends_rows
+            edge_all[side, :, q * lons : (q + 1) * lons] = packed[side * 16 : (side + 1) * 16]
     for step in range(n):
         to = peer(step)
-        right = columns(lax.rem(to + 1, n) * width, LANES)
-        left = columns(lax.rem(to + n - 1, n) * width + width - LANES, LANES)
+        right = lax.rem(to + 1, n) * width
+        left = lax.rem(to + n - 1, n) * width + width - LANES
         for side in range(2):
-            edge_out[side, step, :, :width] = edge_out[side, n, :, columns(to * width, width)]
-            edge_out[side, step, :, width : width + LANES] = jnp.where(
-                near, edge_out[side, n, :, right], edge_out[side, n, :, left]
-            )
+            sides_tile = None
+            for q in range(pairs):
+                edge_out[side, step, :, q * width : (q + 1) * width] = edge_all[
+                    side, :, columns(q * lons + to * width, width)
+                ]
+                after = edge_all[side, :, columns(q * lons + right, LANES)].astype(jnp.float32)
+                before = edge_all[side, :, columns(q * lons + left, LANES)].astype(jnp.float32)
+                if q == 0:
+                    sides_tile = jnp.where(near, after, before)
+                else:
+                    after = pltpu.roll(after, 2 * q, 1)
+                    before = pltpu.roll(before, LANES - 2 * q, 1)
+                    sides_tile = jnp.where((lane >= 2 * q) & near, after, sides_tile)
+                    sides_tile = jnp.where((lane < LANES - 2 * q) & ~near, before, sides_tile)
+            edge_out[side, step, :, pairs * width :] = sides_tile.astype(jnp.bfloat16)
 
     sides = jnp.where(has[0], 1, 0) + jnp.where(has[1], 1, 0)
     pl.semaphore_wait(barrier, n - 1 + n * sides)
 
     def edge_copy(side, step):
         return pltpu.make_async_remote_copy(
-            src_ref=edge_out.at[side, step, :, pl.ds(0, width + LANES)],
+            src_ref=edge_out.at[side, step],
             dst_ref=edge_in.at[1 - side, step],
             send_sem=edge_send.at[side, step],
             recv_sem=edge_recv.at[1 - side, step],
@@ -139,7 +151,7 @@
 
     def edge_arrival(side, step):
         return pltpu.make_async_remote_copy(
-            src_ref=edge_out.at[side, step, :, pl.ds(0, width + LANES)],
+            src_ref=edge_out.at[side, step],
             dst_ref=edge_in.at[side, step],
             send_sem=edge_send.at[side, step],
             recv_sem=edge_recv.at[side, step],
@@ -200,78 +212,67 @@
 
     groups = n * pairs
 
+    def total(term):
+        value = term(0)
+        for p in range(1, groups):
+            value = jax.tree.map(jnp.add, value, term(p))
+        return value
+
+    def slope(e):
+        return east(e) - west(e)
+
+    def x_terms(p, i):
+        e = energy[p, i]
+        gx = slope(e)
+        return e, gx * gx
+
+    def x_moments(i):
+        sums = total(lambda p: x_terms(p, i))
+        first[i], xx[i] = (fold(x, half) for x in sums)
+
     def moments(i):
-        total = sum_xx = sum_xy = sum_yy = None
-        for p in range(groups):
+        def term(p):
             e = energy[p, i]
-            gx = east(e) - west(e)
+            gx = slope(e)
             gy = energy[p, i + 1] - energy[p, i - 1]
-            terms = (e, gx * gx, gx * gy, gy * gy)
-            if p == 0:
-                total, sum_xx, sum_xy, sum_yy = terms
-            else:
-                total, sum_xx, sum_xy, sum_yy = (
-                    total + terms[0], sum_xx + terms[1], sum_xy + terms[2], sum_yy + terms[3]
-                )
-        first[i] = fold(total, half)
-        xx[i] = fold(sum_xx, half)
-        xy[i] = fold(sum_xy, half)
-        yy[i] = fold(sum_yy, half)
-
-    def outer(i):
-        total = sum_xx = None
-        for p in range(groups):
-            e = energy[p, i]
-            gx = east(e) - west(e)
-            total, sum_xx = (e, gx * gx) if p == 0 else (total + e, sum_xx + gx * gx)
-        first[i] = fold(total, half)
-        xx[i] = fold(sum_xx, half)
-
-    pl.loop(2, rows)(moments)
-
-    for side in range(2):
-        row = 0 if side == 0 else rows + 1
-
-        @pl.when(has[side])
-        def _():
-            for step in range(n):
-                edge_arrival(side, step).wait_recv()
-                for q in range(pairs):
-                    parts = edge_in[side, step, q * 16 : (q + 1) * 16, :].astype(jnp.float32)
-                    energy[step * pairs + q, row] = parts[:8] * parts[:8] + parts[8:] * parts[8:]
-
-        @pl.when(jnp.logical_not(has[side]))
-        def _():
-            for p in range(groups):
-                energy[p, row] = jnp.zeros_like(energy[p, row])
-            ends_in[side] = jnp.zeros_like(ends_in[side])
-
-    def ends_copy(side, landing):
+            return e, gx * gx, gx * gy, gy * gy
+
+        first[i], xx[i], xy[i], yy[i] = (fold(x, half) for x in total(term))
+
+    places = ((1, 2, 0, 1.0), (rows, rows - 1, rows + 1, -1.0))
+
+    def remote(source, target, send, recv, side):
         return pltpu.make_async_remote_copy(
-            src_ref=ends_out.at[side],
-            dst_ref=ends_in.at[landing],
-            send_sem=ends_send.at[side],
-            recv_sem=ends_recv.at[landing],
-            device_id={"member": me, "tile": beside[side]},
-            device_id_type=MESH,
-        )
-
-    for side in range(2):
-        row, inner, beyond = (1, 2, 0) if side == 0 else (rows, rows - 1, rows + 1)
-        moments(row)
-        outer(beyond)
-        ends_out[side, 0] = pool(first[row + 1] - first[row - 1], half)
-        ends_out[side, 1] = pool(xy[row], half)
-        ends_out[side, 2] = pool(yy[row], half)
-
-        @pl.when(has[side])
-        def _():
-            ends_copy(side, 1 - side).start()
+            src_ref=source, dst_ref=target, send_sem=send, recv_sem=recv,
+            device_id={"member": me, "tile": beside[side]}, device_id_type=MESH,
+        )
+
+    def early_copy(side, landing):
+        return remote(
+            early_out.at[side], early_in.at[landing], early_send.at[side], early_recv.at[landing], side
+        )
+
+    def late_copy(side, landing):
+        return remote(
+            late_out.at[side], late_in.at[landing], late_send.at[side], late_recv.at[landing], side
+        )
+
+    for side in range(2):
+        row, inner, beyond, sign = places[side]
+        x_moments(row)
+        moments(inner)
+        cross = total(lambda p: slope(energy[p, row]) * energy[p, inner])
+        early_out[side, 0] = pool(first[inner], half)
+        early_out[side, 1] = pool(fold(cross, half), half)
+
+        @pl.when(has[side])
+        def _():
+            early_copy(side, 1 - side).start()
 
     def x_sums(i):
         s = first[i - 1] + first[i] + first[i + 1]
         s = s + west(s) + east(s)
-        return (east(s) - west(s))[:, :half], pool(xx[i - 1] + xx[i] + xx[i + 1], half)
+        return slope(s)[:, :half], pool(xx[i - 1] + xx[i] + xx[i + 1], half)
 
     def inside(i):
         sum_x, sum_xx = x_sums(i)
@@ -280,20 +281,65 @@
         sum_yy = pool(yy[i - 1] + yy[i] + yy[i + 1], half)
         dens[i - 1] = density(sum_x, sum_y, sum_xx, sum_xy, sum_yy, count)
 
-    pl.loop(2, rows)(inside)
-
-    for side in range(2):
-        row, inner = (1, 2) if side == 0 else (rows, rows - 1)
+    pl.loop(3, rows - 1)(moments)
+    pl.loop(3, rows - 1)(inside)
+
+    for side in range(2):
+        row, inner, beyond, sign = places[side]
+
+        @pl.when(has[side])
+        def _():
+            for step in range(n):
+                edge_arrival(side, step).wait_recv()
+                tail = edge_in[side, step, :, pairs * width :].astype(jnp.float32)
+                for q in range(pairs):
+                    parts = edge_in[side, step, :, q * width : (q + 1) * width].astype(jnp.float32)
+                    edge = tail if q == 0 else jnp.where(
+                        near, pltpu.roll(tail, LANES - 2 * q, 1), pltpu.roll(tail, 2 * q, 1)
+                    )
+                    p = step * pairs + q
+                    energy[p, beyond, :, :width] = parts[:8] * parts[:8] + parts[8:] * parts[8:]
+                    energy[p, beyond, :, width:] = edge[:8] * edge[:8] + edge[8:] * edge[8:]
+
+        @pl.when(jnp.logical_not(has[side]))
+        def _():
+            for p in range(groups):
+                energy[p, beyond] = jnp.zeros_like(energy[p, beyond])
+            early_in[side, 0] = pool(first[row], half)
+            early_in[side, 1] = jnp.zeros_like(early_in[side, 1])
+            late_in[side] = jnp.zeros_like(late_in[side])
+
+        def gy_squared(p):
+            gy = energy[p, inner] - energy[p, beyond]
+            return gy * gy
+
+        yy[row] = fold(total(gy_squared), half)
+        late_out[side] = pool(yy[row], half)
+
+        @pl.when(has[side])
+        def _():
+            late_copy(side, 1 - side).start()
+
+    waiting = []
+    for side in range(2):
+        row, inner, beyond, sign = places[side]
+
+        def edge_terms(p):
+            e, other = energy[p, row], energy[p, beyond]
+            gx, gx_other = slope(e), slope(other)
+            gy = sign * (energy[p, inner] - other)
+            return gx * gy, other, gx_other * gx_other, gx_other * e
+
+        xy[row], first[beyond], xx[beyond], cross = (fold(x, half) for x in total(edge_terms))
+        inside(inner)
         sum_x, sum_xx = x_sums(row)
-
-        @pl.when(has[side])
-        def _():
-            ends_copy(side, side).wait_recv()
-
-        sum_y = ends_out[side, 0] + pool(first[inner + 1] - first[inner - 1], half) + ends_in[side, 0]
-        sum_xy = ends_out[side, 1] + pool(xy[inner], half) + ends_in[side, 1]
-        sum_yy = ends_out[side, 2] + pool(yy[inner], half) + ends_in[side, 2]
-        dens[row - 1] = density(sum_x, sum_y, sum_xx, sum_xy, sum_yy, count)
+        sum_y = pool(
+            first[row + 1] - first[row - 1] + first[inner + 1] - first[inner - 1] + sign * first[row],
+            half,
+        )
+        sum_xy = pool(xy[row] + xy[inner] + sign * cross, half)
+        sum_yy = pool(yy[row] + yy[inner], half)
+        waiting.append((sum_x, sum_y, sum_xx, sum_xy, sum_yy))
 
     levels = out.shape[0]
     for r in range(0, rows, 8):
@@ -301,6 +347,23 @@
         out[:, r : r + 8, :half] = turned[:levels]
         out[:, r : r + 8, half:] = turned[levels:]
 
+    for side in range(2):
+        row, inner, beyond, sign = places[side]
+
+        @pl.when(has[side])
+        def _():
+            early_copy(side, side).wait_recv()
+            late_copy(side, side).wait_recv()
+
+        sum_x, sum_y, sum_xx, sum_xy, sum_yy = waiting[side]
+        sum_y = sum_y - sign * early_in[side, 0]
+        sum_xy = sum_xy - sign * early_in[side, 1]
+        sum_yy = sum_yy + late_in[side]
+        edge_row = density(sum_x, sum_y, sum_xx, sum_xy, sum_yy, count)
+        for level in range(levels):
+            out[level, row - 1 : row, :half] = edge_row[level : level + 1]
+            out[level, row - 1 : row, half:] = edge_row[levels + level : levels + level + 1]
+
     for copy in slab_copies + halo_copies:
         copy.wait_send()
     for side in range(2):
@@ -308,7 +371,8 @@
         def _():
             for step in range(n):
                 edge_copy(side, step).wait_send()
-            ends_copy(side, 1 - side).wait_send()
+            early_copy(side, 1 - side).wait_send()
+            late_copy(side, 1 - side).wait_send()
 
 
 def per_device(n, tiles, winds):
@@ -330,21 +394,24 @@
             pltpu.VMEM((pairs * size, lons), jnp.bfloat16),
             pltpu.VMEM((n, pairs * size, width + LANES), jnp.bfloat16),
             pltpu.VMEM((max(n - 1, 1), pairs * size, LANES), jnp.bfloat16),
-            pltpu.VMEM((2, n + 1, pairs * 16, max(lons, width + LANES)), jnp.bfloat16),
-            pltpu.VMEM((2, n, pairs * 16, width + LANES), jnp.bfloat16),
+            pltpu.VMEM((2, 16, pairs * lons), jnp.bfloat16),
+            pltpu.VMEM((2, n, 16, pairs * width + LANES), jnp.bfloat16),
+            pltpu.VMEM((2, n, 16, pairs * width + LANES), jnp.bfloat16),
             pltpu.VMEM((groups, rows + 2, 8, width + LANES), jnp.float32),
             pltpu.VMEM((rows + 2, 8, half + LANES), jnp.float32),
             pltpu.VMEM((rows + 2, 8, half + LANES), jnp.float32),
             pltpu.VMEM((rows + 2, 8, half + LANES), jnp.float32),
             pltpu.VMEM((rows + 2, 8, half + LANES), jnp.float32),
-            pltpu.VMEM((2, 3, 8, half), jnp.float32),
-            pltpu.VMEM((2, 3, 8, half), jnp.float32),
+            pltpu.VMEM((2, 2, 8, half), jnp.float32),
+            pltpu.VMEM((2, 2, 8, half), jnp.float32),
+            pltpu.VMEM((2, 8, half), jnp.float32),
+            pltpu.VMEM((2, 8, half), jnp.float32),
             pltpu.VMEM((rows, 8, half), jnp.float32),
             dma, dma, dma((n,)), dma((n,)), dma((n,)), dma((n,)),
-            dma((2, n)), dma((2, n)), dma((2,)), dma((2,)),
+            dma((2, n)), dma((2, n)), dma((2,)), dma((2,)), dma((2,)), dma((2,)),
         ],
         compiler_params=pltpu.CompilerParams(
-            collective_id=0, has_side_effects=True, vmem_limit_bytes=48 * 2**20
+            collective_id=0, has_side_effects=True, vmem_limit_bytes=60 * 2**20
         ),
     )(winds.reshape(pairs * size, lons))
 

time: 18.4 us -> 17.6 us (0.957)
  the two profiles are of different devices: /device:TPU:13 before, /device:TPU:0 now
where the time goes in v2:
time: 17.6 us; the launch traced here: 17.4 us
  Pallas kernels  15.8 us (90%)
  local copies, waits for them, and re-layouts  1.67 us (9%)
    pallas_call x1, Pallas kernels, per_device(): pl.pallas_call(functools.partial(kernel, n, tiles, rows, pairs, count), o...  15.8 us
    unnamed x1, local copies, waits for them, and re-layouts  1.67 us

profile of v2, /device:TPU:0, one launch (start us, length us, event | category | flops | bytes accessed | tf_op | source)
XLA Modules:
  0.0 17.4 jit_solution(14021663747876857585)
XLA Ops:
  0.0 15.8 %shard_map.17 = f32[4,16,1024]{2,1,0:T(8,128)} custom-call(bf16[512,2048]{1,0:T(8,128)(2,1)} %bitcast.1), custom_call_target="tpu_custom_call" | custom-call | tf_op jit(solution)/shard_map/pallas_call | solution.py:388
  15.8 1.7 %copy.3 = f32[4,16,1024]{2,1,0:T(8,128)} copy(f32[4,16,1024]{2,1,0:T(8,128)} %shard_map.17) | data formatting | bytes 524288

commit v3 on v2

--- a/solution.py
+++ b/solution.py
@@ -66,9 +66,9 @@
 def kernel(
     n, tiles, rows, pairs, count,
     winds, out,
-    own, slab, halo, edge_all, edge_out, edge_in, energy, first, xx, xy, yy,
+    own, slab, halo_out, halo_in, edge_all, edge_out, edge_in, energy, first, xx, xy, yy,
     early_out, early_in, late_out, late_in, dens,
-    own_sem, here_sem, slab_send, slab_recv, halo_send, halo_recv,
+    own_sem, slab_send, slab_recv, halo_send, halo_recv,
     edge_send, edge_recv, early_send, early_recv, late_send, late_recv,
 ):
     me, tile = lax.axis_index("member"), lax.axis_index("tile")
@@ -87,10 +87,6 @@
 
     load = pltpu.make_async_copy(winds, own, own_sem)
     load.start()
-    here = pltpu.make_async_copy(
-        winds.at[:, columns(me * width, width)], slab.at[0, :, pl.ds(0, width)], here_sem
-    )
-    here.start()
 
     barrier = pltpu.get_barrier_semaphore()
     for step in range(1, n):
@@ -136,6 +132,25 @@
                     sides_tile = jnp.where((lane < LANES - 2 * q) & ~near, before, sides_tile)
             edge_out[side, step, :, pairs * width :] = sides_tile.astype(jnp.bfloat16)
 
+    for step in range(n):
+        to = peer(step)
+        right = columns(lax.rem(to + 1, n) * width, LANES)
+        left = columns(lax.rem(to + n - 1, n) * width + width - LANES, LANES)
+        halo_out[step] = jnp.where(near, own[:, right], own[:, left])
+
+    def energies(step, main, halo):
+        for q in range(pairs):
+            here = slice(q * size, (q + 1) * size)
+            for c in range(0, width + LANES, 2 * LANES):
+                chunk = 2 * LANES if c < width else LANES
+                block = main(here, c, chunk) if c < width else halo[here, :]
+                parts = pick(order, block).reshape(rows, 2, 8, chunk)
+                energy[step * pairs + q, 1 : rows + 1, :, c : c + chunk] = (
+                    parts[:, 0] * parts[:, 0] + parts[:, 1] * parts[:, 1]
+                )
+
+    energies(0, lambda here, c, chunk: own[here, columns(me * width + c, chunk)], halo_out.at[0])
+
     sides = jnp.where(has[0], 1, 0) + jnp.where(has[1], 1, 0)
     pl.semaphore_wait(barrier, n - 1 + n * sides)
 
@@ -170,51 +185,26 @@
         device = {"member": peer(step), "tile": tile}
         copy = pltpu.make_async_remote_copy(
             src_ref=winds.at[:, columns(peer(step) * width, width)],
-            dst_ref=slab.at[step, :, pl.ds(0, width)],
+            dst_ref=slab.at[step - 1],
             send_sem=slab_send.at[step], recv_sem=slab_recv.at[step],
             device_id=device, device_id_type=MESH,
         )
         copy.start()
         slab_copies.append(copy)
-
-    for step in range(n):
-        to = peer(step)
-        right = columns(lax.rem(to + 1, n) * width, LANES)
-        left = columns(lax.rem(to + n - 1, n) * width + width - LANES, LANES)
-        tile_columns = jnp.where(near, own[:, right], own[:, left])
-        if step == 0:
-            slab[0, :, width:] = tile_columns
-            continue
-        halo[step - 1] = tile_columns
         copy = pltpu.make_async_remote_copy(
-            src_ref=halo.at[step - 1],
-            dst_ref=slab.at[step, :, pl.ds(width, LANES)],
+            src_ref=halo_out.at[step],
+            dst_ref=halo_in.at[step - 1],
             send_sem=halo_send.at[step], recv_sem=halo_recv.at[step],
-            device_id={"member": to, "tile": tile}, device_id_type=MESH,
+            device_id=device, device_id_type=MESH,
         )
         copy.start()
         halo_copies.append(copy)
 
-    chunk = 3 * LANES if (width + LANES) % (3 * LANES) == 0 else LANES
-    for step in range(n):
-        if step == 0:
-            here.wait()
-        else:
-            slab_copies[step - 1].wait_recv()
-            halo_copies[step - 1].wait_recv()
-        for q in range(pairs):
-            for c in range(0, width + LANES, chunk):
-                block = slab[step, q * size : (q + 1) * size, c : c + chunk]
-                parts = pick(order, block).reshape(rows, 2, 8, chunk)
-                energy[step * pairs + q, 1 : rows + 1, :, c : c + chunk] = (
-                    parts[:, 0] * parts[:, 0] + parts[:, 1] * parts[:, 1]
-                )
-
     groups = n * pairs
 
-    def total(term):
-        value = term(0)
-        for p in range(1, groups):
+    def total(term, start=0, stop=groups):
+        value = term(start)
+        for p in range(start + 1, stop):
             value = jax.tree.map(jnp.add, value, term(p))
         return value
 
@@ -226,18 +216,41 @@
         gx = slope(e)
         return e, gx * gx
 
-    def x_moments(i):
-        sums = total(lambda p: x_terms(p, i))
-        first[i], xx[i] = (fold(x, half) for x in sums)
-
-    def moments(i):
-        def term(p):
-            e = energy[p, i]
-            gx = slope(e)
-            gy = energy[p, i + 1] - energy[p, i - 1]
-            return e, gx * gx, gx * gy, gy * gy
-
-        first[i], xx[i], xy[i], yy[i] = (fold(x, half) for x in total(term))
+    def terms(p, i):
+        e = energy[p, i]
+        gx = slope(e)
+        gy = energy[p, i + 1] - energy[p, i - 1]
+        return e, gx * gx, gx * gy, gy * gy
+
+    def put(targets, i, sums, more):
+        for target, x in zip(targets, sums):
+            x = fold(x, half)
+            target[i] = target[i] + x if more else x
+
+    def x_moments(i, start, stop):
+        put((first, xx), i, total(lambda p: x_terms(p, i), start, stop), start > 0)
+
+    def moments(i, start, stop):
+        put((first, xx, xy, yy), i, total(lambda p: terms(p, i), start, stop), start > 0)
+
+    def band(start, stop):
+        for i in (1, rows):
+            x_moments(i, start, stop)
+        for i in (2, rows - 1):
+            moments(i, start, stop)
+        pl.loop(3, rows - 1, unroll=4)(lambda i: moments(i, start, stop))
+
+    band(0, pairs)
+    for step in range(1, n):
+        slab_copies[step - 1].wait_recv()
+        halo_copies[step - 1].wait_recv()
+        energies(
+            step,
+            lambda here, c, chunk: slab[step - 1, here, c : c + chunk],
+            halo_in.at[step - 1],
+        )
+    if n > 1:
+        band(pairs, groups)
 
     places = ((1, 2, 0, 1.0), (rows, rows - 1, rows + 1, -1.0))
 
@@ -259,8 +272,6 @@
 
     for side in range(2):
         row, inner, beyond, sign = places[side]
-        x_moments(row)
-        moments(inner)
         cross = total(lambda p: slope(energy[p, row]) * energy[p, inner])
         early_out[side, 0] = pool(first[inner], half)
         early_out[side, 1] = pool(fold(cross, half), half)
@@ -281,8 +292,7 @@
         sum_yy = pool(yy[i - 1] + yy[i] + yy[i + 1], half)
         dens[i - 1] = density(sum_x, sum_y, sum_xx, sum_xy, sum_yy, count)
 
-    pl.loop(3, rows - 1)(moments)
-    pl.loop(3, rows - 1)(inside)
+    pl.loop(3, rows - 1, unroll=4)(inside)
 
     for side in range(2):
         row, inner, beyond, sign = places[side]
@@ -392,7 +402,8 @@
         out_specs=pl.BlockSpec(memory_space=pltpu.VMEM),
         scratch_shapes=[
             pltpu.VMEM((pairs * size, lons), jnp.bfloat16),
-            pltpu.VMEM((n, pairs * size, width + LANES), jnp.bfloat16),
+            pltpu.VMEM((max(n - 1, 1), pairs * size, width), jnp.bfloat16),
+            pltpu.VMEM((n, pairs * size, LANES), jnp.bfloat16),
             pltpu.VMEM((max(n - 1, 1), pairs * size, LANES), jnp.bfloat16),
             pltpu.VMEM((2, 16, pairs * lons), jnp.bfloat16),
             pltpu.VMEM((2, n, 16, pairs * width + LANES), jnp.bfloat16),
@@ -407,7 +418,7 @@
             pltpu.VMEM((2, 8, half), jnp.float32),
             pltpu.VMEM((2, 8, half), jnp.float32),
             pltpu.VMEM((rows, 8, half), jnp.float32),
-            dma, dma, dma((n,)), dma((n,)), dma((n,)), dma((n,)),
+            dma, dma((n,)), dma((n,)), dma((n,)), dma((n,)),
             dma((2, n)), dma((2, n)), dma((2,)), dma((2,)), dma((2,)), dma((2,)),
         ],
         compiler_params=pltpu.CompilerParams(

time: 17.6 us -> 17.1 us (0.972)
  Pallas kernels: 15.8 us -> 15.1 us
    pallas_call x1, Pallas kernels: 15.8 us -> 15.1 us  [per_device(): pl.pallas_call(functools.partial(kernel, n, tiles, rows, pairs, count), o...]
where the time goes in v3:
time: 17.1 us; the launch traced here: 16.8 us
  Pallas kernels  15.1 us (88%)
  local copies, waits for them, and re-layouts  1.67 us (10%)
    pallas_call x1, Pallas kernels, per_device(): pl.pallas_call(functools.partial(kernel, n, tiles, rows, pairs, count), o...  15.1 us
    unnamed x1, local copies, waits for them, and re-layouts  1.67 us

profile of v3, /device:TPU:0, one launch (start us, length us, event | category | flops | bytes accessed | tf_op | source)
XLA Modules:
  0.0 16.8 jit_solution(5443313918672670442)
XLA Ops:
  0.0 15.1 %shard_map.17 = f32[4,16,1024]{2,1,0:T(8,128)} custom-call(bf16[512,2048]{1,0:T(8,128)(2,1)} %bitcast.1), custom_call_target="tpu_custom_call" | custom-call | tf_op jit(solution)/shard_map/pallas_call | solution.py:398
  15.1 1.7 %copy.3 = f32[4,16,1024]{2,1,0:T(8,128)} copy(f32[4,16,1024]{2,1,0:T(8,128)} %shard_map.17) | data formatting | bytes 524288

commit v4 on v3

--- a/solution.py
+++ b/solution.py
@@ -85,8 +85,13 @@
     def columns(start, length):
         return pl.ds(pl.multiple_of(start, LANES), length)
 
-    load = pltpu.make_async_copy(winds, own, own_sem)
-    load.start()
+    share = pairs * size // 8
+    loads = []
+    for k in range(8):
+        piece = pl.ds(k * share, share)
+        load = pltpu.make_async_copy(winds.at[piece], own.at[piece], own_sem.at[k])
+        load.start()
+        loads.append(load)
 
     barrier = pltpu.get_barrier_semaphore()
     for step in range(1, n):
@@ -104,7 +109,8 @@
 
     order = row_order(size, rows)
     ends = jnp.concatenate([order[:16], order[size - 16 :]], axis=0)
-    load.wait()
+    for load in loads:
+        load.wait()
     near = lax.broadcasted_iota(jnp.int32, (1, LANES), 1) < LANES // 2
     lane = lax.broadcasted_iota(jnp.int32, (1, LANES), 1)
     for q in range(pairs):
@@ -132,12 +138,6 @@
                     sides_tile = jnp.where((lane < LANES - 2 * q) & ~near, before, sides_tile)
             edge_out[side, step, :, pairs * width :] = sides_tile.astype(jnp.bfloat16)
 
-    for step in range(n):
-        to = peer(step)
-        right = columns(lax.rem(to + 1, n) * width, LANES)
-        left = columns(lax.rem(to + n - 1, n) * width + width - LANES, LANES)
-        halo_out[step] = jnp.where(near, own[:, right], own[:, left])
-
     def energies(step, main, halo):
         for q in range(pairs):
             here = slice(q * size, (q + 1) * size)
@@ -149,8 +149,6 @@
                     parts[:, 0] * parts[:, 0] + parts[:, 1] * parts[:, 1]
                 )
 
-    energies(0, lambda here, c, chunk: own[here, columns(me * width + c, chunk)], halo_out.at[0])
-
     sides = jnp.where(has[0], 1, 0) + jnp.where(has[1], 1, 0)
     pl.semaphore_wait(barrier, n - 1 + n * sides)
 
@@ -180,6 +178,12 @@
             for step in range(n):
                 edge_copy(side, step).start()
 
+    for step in range(n):
+        to = peer(step)
+        right = columns(lax.rem(to + 1, n) * width, LANES)
+        left = columns(lax.rem(to + n - 1, n) * width + width - LANES, LANES)
+        halo_out[step] = jnp.where(near, own[:, right], own[:, left])
+
     slab_copies, halo_copies = [], []
     for step in range(1, n):
         device = {"member": peer(step), "tile": tile}
@@ -240,6 +244,7 @@
             moments(i, start, stop)
         pl.loop(3, rows - 1, unroll=4)(lambda i: moments(i, start, stop))
 
+    energies(0, lambda here, c, chunk: own[here, columns(me * width + c, chunk)], halo_out.at[0])
     band(0, pairs)
     for step in range(1, n):
         slab_copies[step - 1].wait_recv()
@@ -299,17 +304,30 @@
 
         @pl.when(has[side])
         def _():
+            main = tail = None
             for step in range(n):
                 edge_arrival(side, step).wait_recv()
-                tail = edge_in[side, step, :, pairs * width :].astype(jnp.float32)
+                sides_tile = edge_in[side, step, :, pairs * width :].astype(jnp.float32)
                 for q in range(pairs):
+                    p = step * pairs + q
                     parts = edge_in[side, step, :, q * width : (q + 1) * width].astype(jnp.float32)
-                    edge = tail if q == 0 else jnp.where(
-                        near, pltpu.roll(tail, LANES - 2 * q, 1), pltpu.roll(tail, 2 * q, 1)
+                    edge = sides_tile if q == 0 else jnp.where(
+                        near,
+                        pltpu.roll(sides_tile, LANES - 2 * q, 1),
+                        pltpu.roll(sides_tile, 2 * q, 1),
                     )
-                    p = step * pairs + q
-                    energy[p, beyond, :, :width] = parts[:8] * parts[:8] + parts[8:] * parts[8:]
-                    energy[p, beyond, :, width:] = edge[:8] * edge[:8] + edge[8:] * edge[8:]
+                    e = parts[:8] * parts[:8] + parts[8:] * parts[8:]
+                    e_tail = edge[:8] * edge[:8] + edge[8:] * edge[8:]
+                    energy[p, beyond, :, :width] = e
+                    energy[p, beyond, :, width:] = e_tail
+                    gy = energy[p, inner, :, :width] - e
+                    gy_tail = energy[p, inner, :, width:] - e_tail
+                    main = gy * gy if p == 0 else main + gy * gy
+                    tail = gy_tail * gy_tail if p == 0 else tail + gy_tail * gy_tail
+            folded = fold(jnp.concatenate([main, tail], axis=1), half)
+            late_out[side] = pool(folded, half)
+            late_copy(side, 1 - side).start()
+            yy[row] = folded
 
         @pl.when(jnp.logical_not(has[side]))
         def _():
@@ -318,17 +336,9 @@
             early_in[side, 0] = pool(first[row], half)
             early_in[side, 1] = jnp.zeros_like(early_in[side, 1])
             late_in[side] = jnp.zeros_like(late_in[side])
-
-        def gy_squared(p):
-            gy = energy[p, inner] - energy[p, beyond]
-            return gy * gy
-
-        yy[row] = fold(total(gy_squared), half)
-        late_out[side] = pool(yy[row], half)
-
-        @pl.when(has[side])
-        def _():
-            late_copy(side, 1 - side).start()
+            folded = fold(total(lambda p: energy[p, inner] * energy[p, inner]), half)
+            late_out[side] = pool(folded, half)
+            yy[row] = folded
 
     waiting = []
     for side in range(2):
@@ -418,7 +428,7 @@
             pltpu.VMEM((2, 8, half), jnp.float32),
             pltpu.VMEM((2, 8, half), jnp.float32),
             pltpu.VMEM((rows, 8, half), jnp.float32),
-            dma, dma((n,)), dma((n,)), dma((n,)), dma((n,)),
+            dma((8,)), dma((n,)), dma((n,)), dma((n,)), dma((n,)),
             dma((2, n)), dma((2, n)), dma((2,)), dma((2,)), dma((2,)), dma((2,)),
         ],
         compiler_params=pltpu.CompilerParams(

time: 17.1 us -> 16.9 us (0.988)
  the two profiles are of different devices: /device:TPU:0 before, /device:TPU:13 now
where the time goes in v4:
time: 16.9 us; the launch traced here: 16.8 us
  Pallas kernels  15.1 us (89%)
  local copies, waits for them, and re-layouts  1.67 us (10%)
    pallas_call x1, Pallas kernels, per_device(): pl.pallas_call(functools.partial(kernel, n, tiles, rows, pairs, count), o...  15.1 us
    unnamed x1, local copies, waits for them, and re-layouts  1.67 us

profile of v4, /device:TPU:13, one launch (start us, length us, event | category | flops | bytes accessed | tf_op | source)
XLA Modules:
  0.0 16.8 jit_solution(742016482631103307)
XLA Ops:
  0.0 15.1 %shard_map.17 = f32[4,16,1024]{2,1,0:T(8,128)} custom-call(bf16[512,2048]{1,0:T(8,128)(2,1)} %bitcast.1), custom_call_target="tpu_custom_call" | custom-call | tf_op jit(solution)/shard_map/pallas_call | solution.py:408
  15.1 1.7 %copy.3 = f32[4,16,1024]{2,1,0:T(8,128)} copy(f32[4,16,1024]{2,1,0:T(8,128)} %shard_map.17) | data formatting | bytes 524288
